TPU v7x, 32 devices: a whole 2x2x4 slice. The times are simulated.
32 devices in a mesh: rows: 8 (over z, y), cols: 4 (over x, core).
Axes of the slice: x: 2, y: 2, z: 4, core: 2. Of those that a mesh axis runs over, the one named last changes fastest.
Arguments:
- images: bfloat16 [64, 360, 128], P('rows'), may hold values from -8 to 8
- partners: int32 [8, 8], P('rows'), may hold values from 0 to 7, each once within a row
- counts: int32 [8], P('rows'), may hold values from 1 to 8
- start: float32 [8, 24], P('rows'), may hold values from -6 to 6
Outputs:
- first_vec: float32 [8, 24], P('rows')
- second_vec: float32 [8, 24], P('rows')
Inputs may be any that keep to these rules, and one draw needn't show every extreme that they name: Each row of partners lists every code of 0 to 7 once; only its first counts[I] entries are pairs.
All inputs are finite; a program needn't handle non-finite values.
Results may differ from a plain program's by a relative error of at most 0.0003.
Values may be sent and summed in bfloat16 or wider, within the bound.
A program may use at most 64 MiB of HBM per device.

v0:
```python
import math

import jax
import jax.numpy as jnp
from jax import lax
from jax.sharding import PartitionSpec as P

score_gain = 0.4
norm_eps = 1e-06


def shifted(block, axis, distance):
    devices = range(lax.axis_size(axis))
    route = [((i - distance) % len(devices), i) for i in devices]
    return lax.ppermute(block, axis, route)


def line_table(lines):
    angle = 2.0 * math.pi * jnp.arange(lines).astype(jnp.float32) / lines
    return jnp.stack([jnp.cos(angle), jnp.sin(angle), jnp.cos(2.0 * angle)], axis=1)


def pair_tile(own, other, table):
    count, lines, radii = own.shape
    others = other.shape[0]
    flat = other.reshape(others * lines, radii)

    def one_image(lines_a):
        scores = (
            lax.dot_general(
                lines_a, flat, (((1,), (1,)), ((), ())), preferred_element_type=jnp.float32
            )
            * score_gain
        )
        shaped = scores.reshape(lines, others, lines)
        top = jnp.max(shaped, axis=(0, 2))
        weights = jnp.exp(shaped - top[None, :, None])
        total = jnp.sum(weights, axis=(0, 2))
        left = jnp.einsum("lp,lbk->pbk", table, weights, precision=lax.Precision.HIGHEST)
        rel = jnp.einsum("pbk,kq->pbq", left, table, precision=lax.Precision.HIGHEST)
        return rel / total[None, :, None]

    stacked = lax.map(one_image, own)
    return jnp.transpose(stacked, (1, 0, 3, 2)).reshape(3 * count, 3 * others)


def block_offset(code, halo):
    return code - halo if code < halo else code - halo + 1


def body(images, partners, counts, start):
    count, lines, radii = images.shape
    width = 3 * count
    slots = partners.shape[1]
    halo = slots // 2
    ncols = lax.axis_size("cols")
    nblk = lax.axis_size("rows")
    column = lax.axis_index("cols")
    table = line_table(lines)
    share = count // ncols
    own_part = lax.dynamic_slice_in_dim(images, column * share, share, 0)
    fetched = []
    for code in range(2 * halo):
        fetched.append(shifted(own_part, "rows", -block_offset(code, halo)))
    band = jnp.stack(fetched)
    steps = jnp.arange(slots)
    cols_out = 3 * share
    codes = partners[0][steps]
    valid = steps < counts[0]

    def slot_tile(index):
        other = lax.dynamic_index_in_dim(band, codes[index], 0, keepdims=False)
        return lax.cond(
            valid[index],
            lambda: pair_tile(images, other, table),
            lambda: jnp.zeros((width, cols_out), jnp.float32),
        )

    tiles = lax.map(slot_tile, jnp.arange(steps.shape[0]))

    def neighbours(vector):
        pieces = []
        for code in range(2 * halo):
            pieces.append(shifted(vector, "rows", -block_offset(code, halo))[0])
        return jnp.stack(pieces)[codes]

    def apply(vector):
        picked = neighbours(vector)
        shaped = picked.reshape(picked.shape[0], 3, count)
        picked = lax.dynamic_slice_in_dim(shaped, column * share, share, 2).reshape(
            picked.shape[0], cols_out
        )
        products = jnp.einsum("svw,sw->sv", tiles, picked, precision=lax.Precision.HIGHEST)
        partial_value = jnp.sum(jnp.where(valid[:, None], products, 0.0), axis=0)
        return lax.psum(partial_value, "cols").reshape(1, width)

    entries = float(width * nblk)

    def normalize(raw):
        squares = lax.psum(jnp.sum(raw * raw), "rows")
        return raw / jnp.sqrt(squares / entries + norm_eps)

    first_vec = normalize(apply(start))
    second_vec = normalize(apply(first_vec))
    return (first_vec, second_vec)


def solution(mesh):
    in_specs = (P("rows", None, None), P("rows", None), P("rows"), P("rows", None))
    out_specs = (P("rows", None), P("rows", None))
    return jax.shard_map(body, mesh=mesh, in_specs=in_specs, out_specs=out_specs, check_vma=False)
```

profile of v0, /device:TPU:0, one launch (start us, length us, event | category | flops | bytes accessed | tf_op | source)
XLA Modules:
  0.0 441.8 jit_solution(10841012858278854461)
XLA Ops:
  1.6 4.1 collective-permute-start
  5.7 2.5 collective-permute-start.1
  9.1 3.9 collective-permute-start.11
  14.5 5.8 %collective-permute-done.10 = f32[1,24]{1,0:T(1,128)S(1)} collective-permute-done((f32[1,24]{1,0:T(1,128)}, f32[1,24]{1,0:T(1,128)S(1)}, u32[]{:S(2)}, u32[]{:S(2)}) %collective-permute-start.10) | collective-permute-done | bytes 128 | tf_op jit(solution)/shard_map/ppermute | solution.py:15
  20.3 9.0 %collective-permute-start.13 = (f32[1,24]{1,0:T(1,128)}, f32[1,24]{1,0:T(1,128)S(1)}, u32[]{:S(2)}, u32[]{:S(2)}) collective-permute-start(f32[1,24]{1,0:T(1,128)} %param.13), channel_id=1, source_target_pairs={{12,0},{16,4},{20,8},{24,12},{28,16},{0,20},{4,24},{8,28},{13,1},{... | collective-permute-start | bytes 296 | tf_op jit(solution)/shard_map/ppermute | solution.py:15
  29.3 4.1 collective-permute-start.7
  36.5 2.4 collective-permute-done.8
  40.7 2.9 collective-permute-start.4
  44.4 2.4 collective-permute-start.5
  55.4 314.4 %while.26 = (s32[]{:T(128)}, f32[8,24,6]{1,2,0:T(8,128)S(1)}, s32[8]{0:T(128)S(1)}, pred[8]{0:T(512)(128)(4,1)S(1)}, s32[8]{0:T(128)S(1)}, /*index=5*/bf16[8,2,3...) while((s32[]{:T(128)}, f32[8,24,6]{1,2,0:T(8,128)S(1)}, ...), condition=%wide.region_9.10_spmd, body=%wide.region_0.9_spmd.sunk | while | flops 77060184 | bytes 5908325 | solution.py:79
  59.2 35.5 %conditional.2 = (f32[1,24,6]{1,2,0:T(8,128)S(1)}) conditional(s32[]{:T(128)} %bitcast.66, () %tuple.52, (s32[8]{0:T(128)S(1)}, s32[]{:T(128)}, bf16[8,2,360,128]{3,2,1,0:T(8,128)(2,1)}, bf16[8,360,128]{2,1,0:T(8,128)(2,1)}, f32[360,3]{0,1:T(4,128)S(1)}) %tuple.53), branch_computations={%region_1.1_spmd, %region_2.8_spmd} | conditional | flops 77060176 | bytes 5899923 | solution.py:73
  62.7 31.8 %while.25 = (s32[]{:T(128)}, f32[8,3,2,3]{3,2,1,0:T(2,128)S(1)}, bf16[8,360,128]{2,1,0:T(8,128)(2,1)}, bf16[720,128]{1,0:T(8,128)(2,1)S(1)}, f32[360,3]{0,1:T(4,128)S(1)}, /*index=5*/s32[]{:T(128)}, f32[]{:T(128)}, f32[]{:T(128)}) while((s32[]{:T(128)}, f32[8,3,2,3]{3,2,1,0:T(2,128)S(1)}, bf16[8,360,128]{2,1,0:T(8,128)(2,1)}, ...), condition=%wide.region_8.7_spmd, body=%wide.region_3.6_spmd.sunk | while | flops 77060176 | bytes 5528849 | solution.py:43
  98.5 35.5 %conditional.2 = (f32[1,24,6]{1,2,0:T(8,128)S(1)}) conditional(s32[]{:T(128)} %bitcast.66, () %tuple.52, (s32[8]{0:T(128)S(1)}, s32[]{:T(128)}, bf16[8,2,360,128]{3,2,1,0:T(8,128)(2,1)}, bf16[8,360,128]{2,1,0:T(8,128)(2,1)}, f32[360,3]{0,1:T(4,128)S(1)}) %tuple.53), branch_computations={%region_1.1_spmd, %region_2.8_spmd} | conditional | flops 77060176 | bytes 5899923 | solution.py:73
  102.0 31.8 %while.25 = (s32[]{:T(128)}, f32[8,3,2,3]{3,2,1,0:T(2,128)S(1)}, bf16[8,360,128]{2,1,0:T(8,128)(2,1)}, bf16[720,128]{1,0:T(8,128)(2,1)S(1)}, f32[360,3]{0,1:T(4,128)S(1)}, /*index=5*/s32[]{:T(128)}, f32[]{:T(128)}, f32[]{:T(128)}) while((s32[]{:T(128)}, f32[8,3,2,3]{3,2,1,0:T(2,128)S(1)}, bf16[8,360,128]{2,1,0:T(8,128)(2,1)}, ...), condition=%wide.region_8.7_spmd, body=%wide.region_3.6_spmd.sunk | while | flops 77060176 | bytes 5528849 | solution.py:43
  137.8 35.5 %conditional.2 = (f32[1,24,6]{1,2,0:T(8,128)S(1)}) conditional(s32[]{:T(128)} %bitcast.66, () %tuple.52, (s32[8]{0:T(128)S(1)}, s32[]{:T(128)}, bf16[8,2,360,128]{3,2,1,0:T(8,128)(2,1)}, bf16[8,360,128]{2,1,0:T(8,128)(2,1)}, f32[360,3]{0,1:T(4,128)S(1)}) %tuple.53), branch_computations={%region_1.1_spmd, %region_2.8_spmd} | conditional | flops 77060176 | bytes 5899923 | solution.py:73
  141.3 31.8 %while.25 = (s32[]{:T(128)}, f32[8,3,2,3]{3,2,1,0:T(2,128)S(1)}, bf16[8,360,128]{2,1,0:T(8,128)(2,1)}, bf16[720,128]{1,0:T(8,128)(2,1)S(1)}, f32[360,3]{0,1:T(4,128)S(1)}, /*index=5*/s32[]{:T(128)}, f32[]{:T(128)}, f32[]{:T(128)}) while((s32[]{:T(128)}, f32[8,3,2,3]{3,2,1,0:T(2,128)S(1)}, bf16[8,360,128]{2,1,0:T(8,128)(2,1)}, ...), condition=%wide.region_8.7_spmd, body=%wide.region_3.6_spmd.sunk | while | flops 77060176 | bytes 5528849 | solution.py:43
  177.1 35.5 %conditional.2 = (f32[1,24,6]{1,2,0:T(8,128)S(1)}) conditional(s32[]{:T(128)} %bitcast.66, () %tuple.52, (s32[8]{0:T(128)S(1)}, s32[]{:T(128)}, bf16[8,2,360,128]{3,2,1,0:T(8,128)(2,1)}, bf16[8,360,128]{2,1,0:T(8,128)(2,1)}, f32[360,3]{0,1:T(4,128)S(1)}) %tuple.53), branch_computations={%region_1.1_spmd, %region_2.8_spmd} | conditional | flops 77060176 | bytes 5899923 | solution.py:73
  180.6 31.8 %while.25 = (s32[]{:T(128)}, f32[8,3,2,3]{3,2,1,0:T(2,128)S(1)}, bf16[8,360,128]{2,1,0:T(8,128)(2,1)}, bf16[720,128]{1,0:T(8,128)(2,1)S(1)}, f32[360,3]{0,1:T(4,128)S(1)}, /*index=5*/s32[]{:T(128)}, f32[]{:T(128)}, f32[]{:T(128)}) while((s32[]{:T(128)}, f32[8,3,2,3]{3,2,1,0:T(2,128)S(1)}, bf16[8,360,128]{2,1,0:T(8,128)(2,1)}, ...), condition=%wide.region_8.7_spmd, body=%wide.region_3.6_spmd.sunk | while | flops 77060176 | bytes 5528849 | solution.py:43
  216.4 35.5 %conditional.2 = (f32[1,24,6]{1,2,0:T(8,128)S(1)}) conditional(s32[]{:T(128)} %bitcast.66, () %tuple.52, (s32[8]{0:T(128)S(1)}, s32[]{:T(128)}, bf16[8,2,360,128]{3,2,1,0:T(8,128)(2,1)}, bf16[8,360,128]{2,1,0:T(8,128)(2,1)}, f32[360,3]{0,1:T(4,128)S(1)}) %tuple.53), branch_computations={%region_1.1_spmd, %region_2.8_spmd} | conditional | flops 77060176 | bytes 5899923 | solution.py:73
  219.9 31.8 %while.25 = (s32[]{:T(128)}, f32[8,3,2,3]{3,2,1,0:T(2,128)S(1)}, bf16[8,360,128]{2,1,0:T(8,128)(2,1)}, bf16[720,128]{1,0:T(8,128)(2,1)S(1)}, f32[360,3]{0,1:T(4,128)S(1)}, /*index=5*/s32[]{:T(128)}, f32[]{:T(128)}, f32[]{:T(128)}) while((s32[]{:T(128)}, f32[8,3,2,3]{3,2,1,0:T(2,128)S(1)}, bf16[8,360,128]{2,1,0:T(8,128)(2,1)}, ...), condition=%wide.region_8.7_spmd, body=%wide.region_3.6_spmd.sunk | while | flops 77060176 | bytes 5528849 | solution.py:43
  255.7 35.5 %conditional.2 = (f32[1,24,6]{1,2,0:T(8,128)S(1)}) conditional(s32[]{:T(128)} %bitcast.66, () %tuple.52, (s32[8]{0:T(128)S(1)}, s32[]{:T(128)}, bf16[8,2,360,128]{3,2,1,0:T(8,128)(2,1)}, bf16[8,360,128]{2,1,0:T(8,128)(2,1)}, f32[360,3]{0,1:T(4,128)S(1)}) %tuple.53), branch_computations={%region_1.1_spmd, %region_2.8_spmd} | conditional | flops 77060176 | bytes 5899923 | solution.py:73
  259.2 31.8 %while.25 = (s32[]{:T(128)}, f32[8,3,2,3]{3,2,1,0:T(2,128)S(1)}, bf16[8,360,128]{2,1,0:T(8,128)(2,1)}, bf16[720,128]{1,0:T(8,128)(2,1)S(1)}, f32[360,3]{0,1:T(4,128)S(1)}, /*index=5*/s32[]{:T(128)}, f32[]{:T(128)}, f32[]{:T(128)}) while((s32[]{:T(128)}, f32[8,3,2,3]{3,2,1,0:T(2,128)S(1)}, bf16[8,360,128]{2,1,0:T(8,128)(2,1)}, ...), condition=%wide.region_8.7_spmd, body=%wide.region_3.6_spmd.sunk | while | flops 77060176 | bytes 5528849 | solution.py:43
  295.0 35.5 %conditional.2 = (f32[1,24,6]{1,2,0:T(8,128)S(1)}) conditional(s32[]{:T(128)} %bitcast.66, () %tuple.52, (s32[8]{0:T(128)S(1)}, s32[]{:T(128)}, bf16[8,2,360,128]{3,2,1,0:T(8,128)(2,1)}, bf16[8,360,128]{2,1,0:T(8,128)(2,1)}, f32[360,3]{0,1:T(4,128)S(1)}) %tuple.53), branch_computations={%region_1.1_spmd, %region_2.8_spmd} | conditional | flops 77060176 | bytes 5899923 | solution.py:73
  298.5 31.8 %while.25 = (s32[]{:T(128)}, f32[8,3,2,3]{3,2,1,0:T(2,128)S(1)}, bf16[8,360,128]{2,1,0:T(8,128)(2,1)}, bf16[720,128]{1,0:T(8,128)(2,1)S(1)}, f32[360,3]{0,1:T(4,128)S(1)}, /*index=5*/s32[]{:T(128)}, f32[]{:T(128)}, f32[]{:T(128)}) while((s32[]{:T(128)}, f32[8,3,2,3]{3,2,1,0:T(2,128)S(1)}, bf16[8,360,128]{2,1,0:T(8,128)(2,1)}, ...), condition=%wide.region_8.7_spmd, body=%wide.region_3.6_spmd.sunk | while | flops 77060176 | bytes 5528849 | solution.py:43
  334.3 35.5 %conditional.2 = (f32[1,24,6]{1,2,0:T(8,128)S(1)}) conditional(s32[]{:T(128)} %bitcast.66, () %tuple.52, (s32[8]{0:T(128)S(1)}, s32[]{:T(128)}, bf16[8,2,360,128]{3,2,1,0:T(8,128)(2,1)}, bf16[8,360,128]{2,1,0:T(8,128)(2,1)}, f32[360,3]{0,1:T(4,128)S(1)}) %tuple.53), branch_computations={%region_1.1_spmd, %region_2.8_spmd} | conditional | flops 77060176 | bytes 5899923 | solution.py:73
  337.8 31.8 %while.25 = (s32[]{:T(128)}, f32[8,3,2,3]{3,2,1,0:T(2,128)S(1)}, bf16[8,360,128]{2,1,0:T(8,128)(2,1)}, bf16[720,128]{1,0:T(8,128)(2,1)S(1)}, f32[360,3]{0,1:T(4,128)S(1)}, /*index=5*/s32[]{:T(128)}, f32[]{:T(128)}, f32[]{:T(128)}) while((s32[]{:T(128)}, f32[8,3,2,3]{3,2,1,0:T(2,128)S(1)}, bf16[8,360,128]{2,1,0:T(8,128)(2,1)}, ...), condition=%wide.region_8.7_spmd, body=%wide.region_3.6_spmd.sunk | while | flops 77060176 | bytes 5528849 | solution.py:43
  370.1 5.6 %psum.28 = f32[24]{0:T(128)S(1)} all-reduce(f32[24]{0:T(128)S(1)} %select_reduce_fusion.1), channel_id=1, replica_groups=mesh['rows'=8,'cols'=4] {'cols'}, use_global_device_ids=true, to_apply=%region_11.12 | all-reduce | flops 24 | bytes 192 | tf_op jit(solution)/shard_map/psum | solution.py:95
  376.3 22.8 %psum.29 = f32[]{:T(128)} all-reduce(f32[]{:T(128)} %multiply_reduce_fusion.1), channel_id=1, replica_groups=mesh['rows'=8,'cols'=4] {'rows'}, use_global_device_ids=true, to_apply=%region_13.14 | all-reduce | flops 1 | bytes 8 | tf_op jit(solution)/shard_map/psum | solution.py:100
  400.2 4.1 collective-permute-start.17
  404.3 3.3 collective-permute-start.18
  413.7 5.6 %psum.30 = f32[24]{0:T(128)S(1)} all-reduce(f32[24]{0:T(128)S(1)} %select_reduce_fusion), channel_id=1, replica_groups=mesh['rows'=8,'cols'=4] {'cols'}, use_global_device_ids=true, to_apply=%region_15.16 | all-reduce | flops 24 | bytes 192 | tf_op jit(solution)/shard_map/psum | solution.py:95
  419.9 20.7 %psum.31 = f32[]{:T(128)} all-reduce(f32[]{:T(128)} %multiply_reduce_fusion), channel_id=1, replica_groups=mesh['rows'=8,'cols'=4] {'rows'}, use_global_device_ids=true, to_apply=%region_17.18 | all-reduce | flops 1 | bytes 8 | tf_op jit(solution)/shard_map/psum | solution.py:100
  (905 shorter events, 302.0 us)
Async XLA Ops:
  0.6 13.2 %copy-start = (s32[1,8]{1,0:T(1,128)S(1)}, s32[1,8]{1,0:T(1,128)}, u32[]{:S(2)}) copy-start(s32[1,8]{1,0:T(1,128)} %param.11) | copy-start | bytes 100
  1.6 42.8 %collective-permute-start = (bf16[2,360,128]{2,1,0:T(8,128)(2,1)S(1)}, bf16[2,360,128]{2,1,0:T(8,128)(2,1)S(1)}, u32[]{:S(2)}, u32[]{:S(2)}) collective-permute-start(bf16[2,360,128]{2,1,0:T(8,128)(2,1)S(1)} %constant_dynamic-slice_fusion.3), channel_id=1, source_target_pairs={{16,0},{20,4},{24,8},{28,12},{0,16},{4,20},{8,24},{12,28},{17,1},{... | collective-permute-start | bytes 552968 | tf_op jit(solution)/shard_map/ppermute | solution.py:15
  5.7 41.9 %collective-permute-start.1 = (bf16[2,360,128]{2,1,0:T(8,128)(2,1)S(1)}, bf16[2,360,128]{2,1,0:T(8,128)(2,1)S(1)}, u32[]{:S(2)}, u32[]{:S(2)}) collective-permute-start(bf16[2,360,128]{2,1,0:T(8,128)(2,1)S(1)} %constant_dynamic-slice_fusion.3), channel_id=1, source_target_pairs={{20,0},{24,4},{28,8},{0,12},{4,16},{8,20},{12,24},{16,28},{21,1},{... | collective-permute-start | bytes 552968 | tf_op jit(solution)/shard_map/ppermute | solution.py:15
  8.2 40.0 %collective-permute-start.2 = (bf16[2,360,128]{2,1,0:T(8,128)(2,1)S(1)}, bf16[2,360,128]{2,1,0:T(8,128)(2,1)S(1)}, u32[]{:S(2)}, u32[]{:S(2)}) collective-permute-start(bf16[2,360,128]{2,1,0:T(8,128)(2,1)S(1)} %constant_dynamic-slice_fusion.3), channel_id=1, source_target_pairs={{24,0},{28,4},{0,8},{4,12},{8,16},{12,20},{16,24},{20,28},{25,1},{... | collective-permute-start | bytes 552968 | tf_op jit(solution)/shard_map/ppermute | solution.py:15
  8.2 12.1 %collective-permute-start.10 = (f32[1,24]{1,0:T(1,128)}, f32[1,24]{1,0:T(1,128)S(1)}, u32[]{:S(2)}, u32[]{:S(2)}) collective-permute-start(f32[1,24]{1,0:T(1,128)} %param.13), channel_id=1, source_target_pairs={{28,0},{0,4},{4,8},{8,12},{12,16},{16,20},{20,24},{24,28},{29,1},{... | collective-permute-start | bytes 296 | tf_op jit(solution)/shard_map/ppermute | solution.py:15
  9.1 11.3 %collective-permute-start.11 = (f32[1,24]{1,0:T(1,128)}, f32[1,24]{1,0:T(1,128)S(1)}, u32[]{:S(2)}, u32[]{:S(2)}) collective-permute-start(f32[1,24]{1,0:T(1,128)} %param.13), channel_id=1, source_target_pairs={{4,0},{8,4},{12,8},{16,12},{20,16},{24,20},{28,24},{0,28},{5,1},{9... | collective-permute-start | bytes 296 | tf_op jit(solution)/shard_map/ppermute | solution.py:15
  20.3 9.0 %collective-permute-start.12 = (f32[1,24]{1,0:T(1,128)}, f32[1,24]{1,0:T(1,128)S(1)}, u32[]{:S(2)}, u32[]{:S(2)}) collective-permute-start(f32[1,24]{1,0:T(1,128)} %param.13), channel_id=1, source_target_pairs={{8,0},{12,4},{16,8},{20,12},{24,16},{28,20},{0,24},{4,28},{9,1},{1... | collective-permute-start | bytes 296 | tf_op jit(solution)/shard_map/ppermute | solution.py:15
  20.3 13.1 %collective-permute-start.13 = (f32[1,24]{1,0:T(1,128)}, f32[1,24]{1,0:T(1,128)S(1)}, u32[]{:S(2)}, u32[]{:S(2)}) collective-permute-start(f32[1,24]{1,0:T(1,128)} %param.13), channel_id=1, source_target_pairs={{12,0},{16,4},{20,8},{24,12},{28,16},{0,20},{4,24},{8,28},{13,1},{... | collective-permute-start | bytes 296 | tf_op jit(solution)/shard_map/ppermute | solution.py:15
  29.3 5.7 %collective-permute-start.7 = (f32[1,24]{1,0:T(1,128)}, f32[1,24]{1,0:T(1,128)S(1)}, u32[]{:S(2)}, u32[]{:S(2)}) collective-permute-start(f32[1,24]{1,0:T(1,128)} %param.13), channel_id=1, source_target_pairs={{16,0},{20,4},{24,8},{28,12},{0,16},{4,20},{8,24},{12,28},{17,1},{... | collective-permute-start | bytes 296 | tf_op jit(solution)/shard_map/ppermute | solution.py:15
  33.4 5.5 %collective-permute-start.8 = (f32[1,24]{1,0:T(1,128)}, f32[1,24]{1,0:T(1,128)S(1)}, u32[]{:S(2)}, u32[]{:S(2)}) collective-permute-start(f32[1,24]{1,0:T(1,128)} %param.13), channel_id=1, source_target_pairs={{20,0},{24,4},{28,8},{0,12},{4,16},{8,20},{12,24},{16,28},{21,1},{... | collective-permute-start | bytes 296 | tf_op jit(solution)/shard_map/ppermute | solution.py:15
  35.0 5.6 %collective-permute-start.9 = (f32[1,24]{1,0:T(1,128)}, f32[1,24]{1,0:T(1,128)S(1)}, u32[]{:S(2)}, u32[]{:S(2)}) collective-permute-start(f32[1,24]{1,0:T(1,128)} %param.13), channel_id=1, source_target_pairs={{24,0},{28,4},{0,8},{4,12},{8,16},{12,20},{16,24},{20,28},{25,1},{... | collective-permute-start | bytes 296 | tf_op jit(solution)/shard_map/ppermute | solution.py:15
  38.9 10.2 %collective-permute-start.3 = (bf16[2,360,128]{2,1,0:T(8,128)(2,1)S(1)}, bf16[2,360,128]{2,1,0:T(8,128)(2,1)S(1)}, u32[]{:S(2)}, u32[]{:S(2)}) collective-permute-start(bf16[2,360,128]{2,1,0:T(8,128)(2,1)S(1)} %constant_dynamic-slice_fusion.3), channel_id=1, source_target_pairs={{28,0},{0,4},{4,8},{8,12},{12,16},{16,20},{20,24},{24,28},{29,1},{... | collective-permute-start | bytes 552968 | tf_op jit(solution)/shard_map/ppermute | solution.py:15
  40.7 9.1 %collective-permute-start.4 = (bf16[2,360,128]{2,1,0:T(8,128)(2,1)S(1)}, bf16[2,360,128]{2,1,0:T(8,128)(2,1)S(1)}, u32[]{:S(2)}, u32[]{:S(2)}) collective-permute-start(bf16[2,360,128]{2,1,0:T(8,128)(2,1)S(1)} %constant_dynamic-slice_fusion.3), channel_id=1, source_target_pairs={{4,0},{8,4},{12,8},{16,12},{20,16},{24,20},{28,24},{0,28},{5,1},{9... | collective-permute-start | bytes 552968 | tf_op jit(solution)/shard_map/ppermute | solution.py:15
  44.4 7.0 %collective-permute-start.5 = (bf16[2,360,128]{2,1,0:T(8,128)(2,1)S(1)}, bf16[2,360,128]{2,1,0:T(8,128)(2,1)S(1)}, u32[]{:S(2)}, u32[]{:S(2)}) collective-permute-start(bf16[2,360,128]{2,1,0:T(8,128)(2,1)S(1)} %constant_dynamic-slice_fusion.3), channel_id=1, source_target_pairs={{8,0},{12,4},{16,8},{20,12},{24,16},{28,20},{0,24},{4,28},{9,1},{1... | collective-permute-start | bytes 552968 | tf_op jit(solution)/shard_map/ppermute | solution.py:15
  47.6 6.4 %collective-permute-start.6 = (bf16[2,360,128]{2,1,0:T(8,128)(2,1)S(1)}, bf16[2,360,128]{2,1,0:T(8,128)(2,1)S(1)}, u32[]{:S(2)}, u32[]{:S(2)}) collective-permute-start(bf16[2,360,128]{2,1,0:T(8,128)(2,1)S(1)} %constant_dynamic-slice_fusion.3), channel_id=1, source_target_pairs={{12,0},{16,4},{20,8},{24,12},{28,16},{0,20},{4,24},{8,28},{13,1},{... | collective-permute-start | bytes 552968 | tf_op jit(solution)/shard_map/ppermute | solution.py:15
  399.8 42.0 %copy-start.1 = (f32[1,24]{1,0:T(1,128)}, f32[1,24]{1,0:T(1,128)S(1)}, u32[]{:S(2)}) copy-start(f32[1,24]{1,0:T(1,128)S(1)} %divide_bitcast_fusion.1) | copy-start | bytes 292
  399.8 7.7 %collective-permute-start.14 = (f32[1,24]{1,0:T(1,128)S(1)}, f32[1,24]{1,0:T(1,128)S(1)}, u32[]{:S(2)}, u32[]{:S(2)}) collective-permute-start(f32[1,24]{1,0:T(1,128)S(1)} %divide_bitcast_fusion.1), channel_id=1, source_target_pairs={{16,0},{20,4},{24,8},{28,12},{0,16},{4,20},{8,24},{12,28},{17,1},{... | collective-permute-start | bytes 296 | tf_op jit(solution)/shard_map/ppermute | solution.py:15
  399.9 8.2 %collective-permute-start.15 = (f32[1,24]{1,0:T(1,128)S(1)}, f32[1,24]{1,0:T(1,128)S(1)}, u32[]{:S(2)}, u32[]{:S(2)}) collective-permute-start(f32[1,24]{1,0:T(1,128)S(1)} %divide_bitcast_fusion.1), channel_id=1, source_target_pairs={{20,0},{24,4},{28,8},{0,12},{4,16},{8,20},{12,24},{16,28},{21,1},{... | collective-permute-start | bytes 296 | tf_op jit(solution)/shard_map/ppermute | solution.py:15
  400.2 7.9 %collective-permute-start.16 = (f32[1,24]{1,0:T(1,128)S(1)}, f32[1,24]{1,0:T(1,128)S(1)}, u32[]{:S(2)}, u32[]{:S(2)}) collective-permute-start(f32[1,24]{1,0:T(1,128)S(1)} %divide_bitcast_fusion.1), channel_id=1, source_target_pairs={{24,0},{28,4},{0,8},{4,12},{8,16},{12,20},{16,24},{20,28},{25,1},{... | collective-permute-start | bytes 296 | tf_op jit(solution)/shard_map/ppermute | solution.py:15
  400.2 8.9 %collective-permute-start.17 = (f32[1,24]{1,0:T(1,128)S(1)}, f32[1,24]{1,0:T(1,128)S(1)}, u32[]{:S(2)}, u32[]{:S(2)}) collective-permute-start(f32[1,24]{1,0:T(1,128)S(1)} %divide_bitcast_fusion.1), channel_id=1, source_target_pairs={{28,0},{0,4},{4,8},{8,12},{12,16},{16,20},{20,24},{24,28},{29,1},{... | collective-permute-start | bytes 296 | tf_op jit(solution)/shard_map/ppermute | solution.py:15
  404.3 4.8 %collective-permute-start.18 = (f32[1,24]{1,0:T(1,128)S(1)}, f32[1,24]{1,0:T(1,128)S(1)}, u32[]{:S(2)}, u32[]{:S(2)}) collective-permute-start(f32[1,24]{1,0:T(1,128)S(1)} %divide_bitcast_fusion.1), channel_id=1, source_target_pairs={{4,0},{8,4},{12,8},{16,12},{20,16},{24,20},{28,24},{0,28},{5,1},{9... | collective-permute-start | bytes 296 | tf_op jit(solution)/shard_map/ppermute | solution.py:15
  407.5 3.5 collective-permute-start.19
  408.1 4.4 %collective-permute-start.20 = (f32[1,24]{1,0:T(1,128)S(1)}, f32[1,24]{1,0:T(1,128)S(1)}, u32[]{:S(2)}, u32[]{:S(2)}) collective-permute-start(f32[1,24]{1,0:T(1,128)S(1)} %divide_bitcast_fusion.1), channel_id=1, source_target_pairs={{12,0},{16,4},{20,8},{24,12},{28,16},{0,20},{4,24},{8,28},{13,1},{... | collective-permute-start | bytes 296 | tf_op jit(solution)/shard_map/ppermute | solution.py:15
where the time goes:
time: 445 us; the launch traced here: 442 us
  matrix products  149 us (33%)
  local copies, waits for them, and re-layouts  109 us (24%)
  blocking collectives  54.7 us (12%)
  starting transfers between devices  42.3 us (10%)
  loops' own time  37.8 us (8%)
  other arithmetic  29.9 us (7%)
  waiting for transfers between devices  16.4 us (4%)
    dot_general x64, matrix products, one_image(): lax.dot_general(lines_a, flat, (((1,), (1,)), ((), ())), preferred_elemen...  81 us
    reshape x64, local copies, waits for them, and re-layouts, one_image(): shaped = scores.reshape(lines, others, lines)  55.3 us
    dot_general x64, matrix products, one_image(): jnp.einsum('lp,lbk->pbk', table, weights, precision=lax.Precision.HIGHEST)  54.2 us
    psum x2, blocking collectives, normalize(): squares = lax.psum(jnp.sum(raw * raw), 'rows')  43.4 us
    ppermute x21, starting transfers between devices, shifted(): return lax.ppermute(block, axis, route)  42.3 us
    another operation x1, loops' own time, body(): tiles = lax.map(slot_tile, jnp.arange(steps.shape[0]))  20.6 us
    reduce_sum x128, other arithmetic, one_image(): total = jnp.sum(weights, axis=(0, 2))  20 us
    ppermute x21, waiting for transfers between devices, shifted(): return lax.ppermute(block, axis, route)  16.4 us
  transfers between devices with their start and end apart: 21, of which 9 were waited for; matrix products, arithmetic and copies ran while one was open for 1% of the time, Pallas kernels for 0%

commit v1 on v0

v1 whole, which is shorter than its diff:
```python
import functools
import math

import jax
import jax.numpy as jnp
import numpy as np
from jax import lax
from jax.experimental import pallas as pl
from jax.experimental.pallas import tpu as pltpu
from jax.sharding import PartitionSpec as P

score_gain = 0.4
norm_eps = 1e-06
MESH = pl.DeviceIdType.MESH
HIGHEST = lax.Precision.HIGHEST


def line_order(lines):
    half, quarter = lines // 2, lines // 4
    rows = (quarter + 1 + 7) // 8 * 8
    order = np.zeros((4, rows), np.int32)
    real = np.zeros((4, rows), np.float32)
    base = list(range(1, quarter + 1)) + [0]
    for r in range(rows):
        g = base[r] if r < len(base) else 0
        order[:, r] = [g, half - g, half + g, (lines - g) % lines]
        if r < len(base):
            real[:, r] = 1.0 if 0 < g < quarter else [1.0, 0.0, 1.0, 0.0]
    angle = np.zeros(rows)
    angle[: len(base)] = 2.0 * math.pi * np.array(base) / lines
    return order, real, angle


def constants(lines, width):
    order, real, angle = line_order(lines)
    rows = order.shape[1]
    pick = np.zeros((4 * rows, lines), np.float32)
    pick[np.arange(4 * rows), order.reshape(-1)] = 1.0
    pad = np.zeros((width, lines), np.float32)
    pad[np.arange(lines), np.arange(lines)] = 1.0
    coef = np.stack([np.cos(angle), np.sin(angle), np.cos(2.0 * angle)])
    coef = np.broadcast_to(coef[:, :, None], (3, rows, 128)).astype(np.float32)
    keep = np.broadcast_to(real[:, rows - 8 :, None], (4, 8, 128)).astype(np.float32)
    t = 2.0 * math.pi * np.arange(lines) / lines
    table = np.zeros((2, 8, width), np.float32)
    table[0, 0:3, :lines] = [np.cos(t), np.sin(t), np.cos(2.0 * t)]
    table[1, 3:6, :lines] = table[0, 0:3, :lines]
    table[1, 6, :lines] = 1.0
    return pick, pad, coef, keep, table


def kernel(
    nblk, ncols, lines,
    counts_ref, partners_ref, start_ref, images_ref, pick_ref, pad_ref, coef_ref, keep_ref, table_ref,
    out_ref,
    recv, own, other, s0, s1, s2, s3, left, packet, send_sem, recv_sem, psend_sem, precv_sem,
):
    scores = (s0, s1, s2, s3)
    count = images_ref.shape[0]
    share = count // ncols
    fetch = recv.shape[0]
    halo = fetch // share
    slots = partners_ref.shape[1]
    width = other.shape[0]
    rows = own.shape[1] // 4
    half_images = count // 2
    row = lax.axis_index("rows")
    col = lax.axis_index("cols")
    me = row * ncols + col
    total = nblk * ncols
    ring = nblk == 2 * halo

    sends = []
    for k in range(1, halo + 1):
        for b in range(share):
            f = (k - 1) * share + b
            target = lax.rem(row - k + nblk, nblk)
            copy = pltpu.make_async_remote_copy(
                src_ref=images_ref.at[col * share + b],
                dst_ref=recv.at[f],
                send_sem=send_sem.at[f],
                recv_sem=recv_sem.at[f],
                device_id=(target, col),
                device_id_type=MESH,
            )
            copy.start()
            sends.append(copy)

    left[...] = jnp.zeros_like(left)

    @pl.loop(0, count)
    def _(a):
        own[a] = jnp.dot(
            pick_ref[...], images_ref[a], preferred_element_type=jnp.float32
        ).astype(jnp.bfloat16)

    scale = score_gain * math.log2(math.e)
    lane = lax.broadcasted_iota(jnp.int32, (8, width), 1)
    side = jnp.where(row >= nblk // 2, 1, 0)
    high = jnp.where(col >= ncols // 2, 1, 0)
    mixed = lax.rem(side + high, 2)
    split = fetch - share if ring else fetch
    units = 2 * split + (fetch - split)

    def unit(u, carry):
        f = jnp.where(u < 2 * split, u // 2, u - split)
        h = jnp.where(u < 2 * split, lax.rem(u, 2), mixed)
        fresh = jnp.where(u < 2 * split, 1 - lax.rem(u, 2), 1)

        @pl.when(fresh == 1)
        def _():
            pltpu.make_async_copy(recv.at[f], recv.at[f], recv_sem.at[f]).wait()
            other[...] = jnp.dot(
                pad_ref[...], recv[f], preferred_element_type=jnp.float32
            ).astype(jnp.bfloat16)

        for i in range(half_images):
            s_ref = scores[i]
            a = h * half_images + i
            s = lax.dot_general(
                own[a], other[...], (((1,), (1,)), ((), ())), preferred_element_type=jnp.float32
            )
            s_ref[...] = s
            top = jnp.max(s.reshape(4 * rows // 8, 8, width), axis=0)
            acc = [jnp.zeros((8, width), jnp.float32) for _ in range(4)]
            for g in range(rows // 8):
                w = []
                for j in range(4):
                    part = s_ref[j * rows + g * 8 : j * rows + g * 8 + 8, :]
                    part = jnp.exp2((part - top) * scale)
                    if g == rows // 8 - 1:
                        part = part * keep_ref[j][:, 0:1]
                    w.append(part)
                s14, d14 = w[0] + w[3], w[0] - w[3]
                s23, d23 = w[1] + w[2], w[1] - w[2]
                both = s14 + s23
                at = slice(g * 8, g * 8 + 8)
                acc[0] = acc[0] + (s14 - s23) * coef_ref[0, at, 0:1]
                acc[1] = acc[1] + (d14 + d23) * coef_ref[1, at, 0:1]
                acc[2] = acc[2] + both * coef_ref[2, at, 0:1]
                acc[3] = acc[3] + both
            masked = jnp.where(lane < lines, top, -jnp.inf)
            peak = jnp.max(masked)
            factor = jnp.exp2((masked - peak) * scale)
            for p in range(4):
                left[p, pl.ds(f * count + a, 1), :] = jnp.sum(acc[p] * factor, axis=0, keepdims=True)
        return carry

    lax.fori_loop(0, units, unit, 0)

    npair = fetch * count
    nt = (((1,), (1,)), ((), ()))
    first = lax.dot_general(
        table_ref[0], left[0:2].reshape(2 * npair, width), nt, precision=HIGHEST,
        preferred_element_type=jnp.float32,
    )
    second = lax.dot_general(
        table_ref[1], left[2:4].reshape(2 * npair, width), nt, precision=HIGHEST,
        preferred_element_type=jnp.float32,
    )
    sums = second[6:7, npair:]
    sums = jnp.concatenate([sums, sums], axis=1)
    inverse = jnp.where(sums > 0.0, 1.0 / sums, 0.0)
    prow = lax.broadcasted_iota(jnp.int32, (8, 2 * npair), 0)
    plane = lax.broadcasted_iota(jnp.int32, (8, 2 * npair), 1)
    value = jnp.where(prow < 3, first, jnp.where(prow < 6, second, 0.0)) * inverse
    valid = jnp.zeros((8, 2 * npair), jnp.float32)
    for s in range(slots):
        on = jnp.where(counts_ref[0] > s, 1.0, 0.0)
        valid = valid + jnp.where(plane == partners_ref[0, s], on, 0.0)
    packet[...] = jnp.where(prow == 6, valid, value)
    packet[7:8, :] = jnp.zeros((1, 2 * npair), jnp.float32)
    packet[7:8, 0 : start_ref.shape[1]] = start_ref[...]
    out_ref[me] = packet[...]

    def give(t, carry):
        target = lax.rem(me + t, total)
        pltpu.make_async_remote_copy(
            src_ref=packet,
            dst_ref=out_ref.at[me],
            send_sem=psend_sem,
            recv_sem=precv_sem,
            device_id=(target // ncols, lax.rem(target, ncols)),
            device_id_type=MESH,
        ).start()
        return carry

    lax.fori_loop(1, total, give, 0)
    for copy in sends:
        copy.wait_send()
    everyone = out_ref.at[pl.ds(0, total - 1)]
    pltpu.make_async_copy(everyone, everyone, psend_sem).wait()
    pltpu.make_async_copy(everyone, everyone, precv_sem).wait()


def body(images, partners, counts, start):
    count, lines, radii = images.shape
    slots = partners.shape[1]
    halo = slots // 2
    ncols = lax.axis_size("cols")
    nblk = lax.axis_size("rows")
    share = count // ncols
    width = (lines + 127) // 128 * 128
    pick, pad, coef, keep, table = constants(lines, width)
    rows4 = pick.shape[0]
    total = nblk * ncols
    npair = halo * share * count
    vmem = pl.BlockSpec(memory_space=pltpu.VMEM)
    smem = pl.BlockSpec(memory_space=pltpu.SMEM)
    packets = pl.pallas_call(
        functools.partial(kernel, nblk, ncols, lines),
        out_shape=jax.ShapeDtypeStruct((total, 8, 2 * npair), jnp.float32),
        in_specs=[smem, smem] + [vmem] * 7,
        out_specs=vmem,
        scratch_shapes=[
            pltpu.VMEM((halo * share, lines, radii), jnp.bfloat16),
            pltpu.VMEM((count, rows4, radii), jnp.bfloat16),
            pltpu.VMEM((width, radii), jnp.bfloat16),
            pltpu.VMEM((rows4, width), jnp.float32),
            pltpu.VMEM((rows4, width), jnp.float32),
            pltpu.VMEM((rows4, width), jnp.float32),
            pltpu.VMEM((rows4, width), jnp.float32),
            pltpu.VMEM((4, npair, width), jnp.float32),
            pltpu.VMEM((8, 2 * npair), jnp.float32),
            pltpu.SemaphoreType.DMA((halo * share,)),
            pltpu.SemaphoreType.DMA((halo * share,)),
            pltpu.SemaphoreType.DMA,
            pltpu.SemaphoreType.DMA,
        ],
        compiler_params=pltpu.CompilerParams(has_side_effects=True, vmem_limit_bytes=40 * 2**20),
    )(
        counts, partners, start, images,
        jnp.asarray(pick, jnp.bfloat16), jnp.asarray(pad, jnp.bfloat16),
        jnp.asarray(coef), jnp.asarray(keep), jnp.asarray(table),
    )

    rel = jnp.stack(
        [packets[:, 0:3, :npair], packets[:, 0:3, npair:], packets[:, 3:6, :npair]], axis=1
    ).reshape(nblk, ncols, 3, 3, halo, share, count)
    chosen = packets[::ncols, 6, :slots]
    ahead = chosen[:, halo:]
    behind = chosen[:, :halo][:, ::-1]
    if nblk == 2 * halo:
        ahead = ahead.at[:, -1].add(chosen[:, 0])
        behind = behind.at[:, -1].add(chosen[:, -1])
    vector = packets[::ncols, 7, : 3 * count].reshape(nblk, 3, count)

    def apply(x):
        split = x.reshape(nblk, 3, ncols, share)
        near = jnp.stack([jnp.roll(split, -k, axis=0) for k in range(1, halo + 1)], axis=1)
        near = near * ahead[:, :, None, None, None]
        forward = jnp.einsum("icpqkba,ikqcb->ipa", rel, near, precision=HIGHEST)
        back = jnp.einsum("icpqkba,ipa->ikqcb", rel, x, precision=HIGHEST)
        result = forward
        for k in range(1, halo + 1):
            term = jnp.roll(back[:, k - 1], k, axis=0) * behind[:, k - 1][:, None, None, None]
            result = result + term.reshape(nblk, 3, count)
        return result

    def normalize(raw):
        return raw / jnp.sqrt(jnp.mean(raw * raw) + norm_eps)

    one = normalize(apply(vector))
    two = normalize(apply(one))
    row = lax.axis_index("rows")

    def mine(x):
        return lax.dynamic_slice_in_dim(x.reshape(nblk, 3 * count), row, 1, 0)

    return mine(one), mine(two)


def solution(mesh):
    in_specs = (P("rows", None, None), P("rows", None), P("rows"), P("rows", None))
    out_specs = (P("rows", None), P("rows", None))
    return jax.shard_map(body, mesh=mesh, in_specs=in_specs, out_specs=out_specs, check_vma=False)
```

time: 445 us -> 105 us (0.24)
  matrix products: 149 us -> 41.5 us
  local copies, waits for them, and re-layouts: 109 us -> 13.7 us
  blocking collectives: 54.7 us -> 0 us
  starting transfers between devices: 42.3 us -> 0 us
  Pallas kernels: 0 us -> 41.6 us
  loops' own time: 37.8 us -> 0 us
  other arithmetic: 29.9 us -> 4.59 us
  waiting for transfers between devices: 16.4 us -> 0 us
    dot_general x194 -> x1, matrix products: 149 us -> 41.5 us  [apply(): back = jnp.einsum('icpqkba,ipa->ikqcb', rel, x, precision=HIGHEST)]
    reshape x68 -> x0, local copies, waits for them, and re-layouts: 55.6 us -> none  [the longest x64 55.3 us: one_image(): shaped = scores.reshape(lines, others, lines)]
    psum x4 -> x0, blocking collectives: 54.7 us -> none  [the longest x2 43.4 us: normalize(): squares = lax.psum(jnp.sum(raw * raw), 'rows')]
    ppermute x21 -> x0, starting transfers between devices: 42.3 us -> none  [shifted(): return lax.ppermute(block, axis, route)]
    pallas_call x0 -> x1, Pallas kernels: none -> 41.6 us  [body(): pl.pallas_call(functools.partial(kernel, nblk, ncols, lines), out_shape=j...]
    another operation x17 -> x0, loops' own time: 37.8 us -> none  [the longest x1 20.6 us: body(): tiles = lax.map(slot_tile, jnp.arange(steps.shape[0]))]
    dynamic_slice x35 -> x2, local copies, waits for them, and re-layouts: 23.7 us -> 0.15 us  [mine(): return lax.dynamic_slice_in_dim(x.reshape(nblk, 3 * count), row, 1, 0)]
    reduce_sum x132 -> x2, other arithmetic: 21.4 us -> 1.4 us  [normalize(): return raw / jnp.sqrt(jnp.mean(raw * raw) + norm_eps)]
  transfers between devices with their start and end apart: 21 -> 0, of which waited for: 9 -> 0; matrix products, arithmetic and copies ran while one was open for 1% -> 0% of each run, Pallas kernels for 0% -> 0%
where the time goes in v1:
time: 105 us; the launch traced here: 104 us
  Pallas kernels  41.6 us (40%)
  matrix products  41.5 us (40%)
  local copies, waits for them, and re-layouts  13.7 us (13%)
  other arithmetic  4.59 us (4%)
  between operations  2.89 us (3%)
    pallas_call x1, Pallas kernels, body(): pl.pallas_call(functools.partial(kernel, nblk, ncols, lines), out_shape=j...  41.6 us
    dot_general x1, matrix products, apply(): back = jnp.einsum('icpqkba,ipa->ikqcb', rel, x, precision=HIGHEST)  41.5 us
    unnamed x23, local copies, waits for them, and re-layouts  8.75 us
    unnamed x6, other arithmetic  2.42 us

profile of v1, /device:TPU:0, one launch (start us, length us, event | category | flops | bytes accessed | tf_op | source)
XLA Modules:
  0.0 104.3 jit_solution(11303297631088777364)
XLA Ops:
  1.3 1.1 %copy-done = bf16[8,360,128]{2,1,0:T(8,128)(2,1)S(1)} copy-done((bf16[8,360,128]{2,1,0:T(8,128)(2,1)S(1)}, bf16[8,360,128]{2,1,0:T(8,128)(2,1)}, u32[]{:S(2)}) %copy-start) | copy-done | bytes 737304
  2.4 1.0 copy-done.1
  3.4 1.0 copy-done.2
  4.3 0.9 copy-done.3
  5.2 0.7 copy-done.4
  6.0 0.7 copy-done.5
  6.7 0.7 copy-done.6
  7.3 0.7 copy-done.7
  8.0 41.6 %shard_map.104 = f32[32,8,128]{2,1,0:T(8,128)S(1)} custom-call(s32[1]{0:T(128)S(6)} %copy.111.counts_ref, s32[1,8]{1,0:T(1,128)S(1)} %copy-done.6, f32[1,24]{1,0:T(1,128)S(1)} %copy-done.7, bf16[8,360,128]{2,1,0:T(8,128)(2,1)S(1)} %copy-done, bf16[384,360]{1,0:T(8,128)(2,1)S(1)} %copy-done.1, bf16[384,360]{1,0:T(8,128)(2,1)S(1)} %copy-done.2, ...), custom_call_target="tpu_custom_call" | custom-call | tf_op jit(solution)/shard_map/pallas_call | solution.py:210
  49.6 0.2 slice_reduce_fusion.2
  49.9 0.1 fusion.16
  50.1 0.5 stack.42
  50.7 0.5 stack.43
  51.3 0.5 stack.44
  51.9 41.5 %fusion = f32[8,1,4,3,4,2,1]{5,1,6,4,3,2,0:T(1,128)S(1)} fusion(f32[8,3,8,1,1,1,1]{2,3,1,6,5,4,0:T(1,128)S(1)} %reshape.158, f32[8,4,3,3,4,2,8]{6,5,4,1,0,3,2:T(2,128)S(1)} %constant_dynamic-update-slice_fusion), kind=kOutput, calls=%fused_computation.3 | convolution fusion | flops 221184 | bytes 77568 | tf_op jit(solution)/shard_map/icpqkba,ipa->ikqcb/dot_general | solution.py:253
  93.4 0.4 copy.76
  94.1 0.1 copy.92
  94.2 0.1 copy.44
  94.3 0.1 copy.47
  94.4 0.1 maximum_bitcast_fusion.2
  94.6 0.1 slice.337
  94.9 0.1 maximum_bitcast_fusion
  95.3 0.4 copy.101
  95.7 0.7 multiply_reduce_fusion.2
  96.6 0.7 multiply_reduce_fusion.4
  98.1 0.6 copy.99
  98.7 0.9 multiply_reduce_fusion
  99.6 0.4 copy.90
  100.9 0.4 copy.102
  101.3 0.7 multiply_reduce_fusion.1
  102.2 0.7 multiply_reduce_fusion.3
  103.7 0.6 copy.100
  (64 shorter events, 2.6 us)
Async XLA Ops:
  1.3 1.1 %copy-start = (bf16[8,360,128]{2,1,0:T(8,128)(2,1)S(1)}, bf16[8,360,128]{2,1,0:T(8,128)(2,1)}, u32[]{:S(2)}) copy-start(bf16[8,360,128]{2,1,0:T(8,128)(2,1)} %images_ref.1) | copy-start | bytes 2211844
  2.4 1.0 copy-start.1
  3.4 1.0 copy-start.2
  4.3 0.9 copy-start.3
  5.2 0.7 copy-start.4
  6.0 0.7 copy-start.5
  6.7 0.7 copy-start.6
  7.3 0.7 copy-start.7

commit v2 on v1

v2 whole, which is shorter than its diff:
```python
import functools
import math

import jax
import jax.numpy as jnp
import numpy as np
from jax import lax
from jax.experimental import pallas as pl
from jax.experimental.pallas import tpu as pltpu
from jax.sharding import PartitionSpec as P

score_gain = 0.4
norm_eps = 1e-06
MESH = pl.DeviceIdType.MESH
HIGHEST = lax.Precision.HIGHEST


def line_order(lines):
    half, quarter = lines // 2, lines // 4
    rows = (quarter + 1 + 7) // 8 * 8
    order = np.zeros((4, rows), np.int32)
    real = np.zeros((4, rows), np.float32)
    base = list(range(1, quarter + 1)) + [0]
    for r in range(rows):
        g = base[r] if r < len(base) else 0
        order[:, r] = [g, half - g, half + g, (lines - g) % lines]
        if r < len(base):
            real[:, r] = 1.0 if 0 < g < quarter else [1.0, 0.0, 1.0, 0.0]
    angle = np.zeros(rows)
    angle[: len(base)] = 2.0 * math.pi * np.array(base) / lines
    return order, real, angle


def constants(lines, width):
    order, real, angle = line_order(lines)
    rows = order.shape[1]
    coef = np.stack([np.cos(angle), np.sin(angle), np.cos(2.0 * angle)])
    coef = np.broadcast_to(coef[:, :, None], (3, rows, 128)).reshape(-1, 128)
    keep = np.broadcast_to(real[:, rows - 8 :, None], (4, 8, 128)).reshape(-1, 128)
    t = 2.0 * math.pi * np.arange(lines) / lines
    table = np.zeros((2, 8, width), np.float32)
    table[0, 0:3, :lines] = [np.cos(t), np.sin(t), np.cos(2.0 * t)]
    table[1, 3:6, :lines] = table[0, 0:3, :lines]
    table[1, 6, :lines] = 1.0
    pick = np.broadcast_to(order.reshape(-1)[:, None], (4 * rows, 128))
    return np.concatenate([coef, keep, table.reshape(-1, 128), pick]).astype(np.float32)


def iota(shape, axis):
    return lax.broadcasted_iota(jnp.int32, shape, axis)


def onehot(condition, dtype=jnp.float32):
    return jnp.where(condition, 1.0, 0.0).astype(dtype)


def product(left, right):
    return jnp.dot(left, right, precision=HIGHEST, preferred_element_type=jnp.float32)


def product_nt(left, right):
    return lax.dot_general(
        left, right, (((1,), (1,)), ((), ())), precision=HIGHEST, preferred_element_type=jnp.float32
    )


def iterate(gathered, nblk, ncols, halo, share, count, slots):
    total = nblk * ncols
    ring = nblk == 2 * halo
    npair = halo * share * count
    lanes = 2 * npair
    entries = 3 * count
    picks = [gathered[:, q, :] for q in range(8)]
    zero = onehot(iota((nblk, total), 1) == iota((nblk, total), 0) * ncols)
    chosen = product(zero, picks[6])
    start = product(zero, picks[7])
    at = iota((1, lanes), 1)
    at_k = (at % npair) // (share * count)
    place = (halo + 1) * total
    k = iota((place, nblk), 0) // total
    block = iota((place, nblk), 0) % total // ncols
    step = jnp.where(k < halo, k + 1, 0)
    spread = onehot(iota((place, nblk), 1) == (block + step) % nblk)
    entry = iota((total, 128), 1)
    owner = iota((total, 128), 0) % ncols
    mine = onehot((entry < entries) & (entry % count // share == owner))
    r, c = iota((128, 3 * lanes), 0), iota((128, 3 * lanes), 1)
    far = onehot(
        (r < entries) & (r // count == c // lanes) & (r % share == c % lanes % (share * count) // count)
    )
    r, c = iota((128, 2 * lanes), 0), iota((128, 2 * lanes), 1)
    part = c // npair
    near = onehot((r < entries) & (r % count == c % count) & (r // count == part))
    code, k2 = iota((128, lanes), 0), iota((128, lanes), 1) % npair // (share * count)
    ahead = code == halo + k2
    behind = code == halo - 1 - k2
    if ring:
        ahead = ahead | ((code == 0) & (k2 == halo - 1))
        behind = behind | ((code == slots - 1) & (k2 == halo - 1))
    here = product(spread[halo * total :], chosen)
    weight_near = product(here, onehot(ahead))
    others = product(product(spread[: halo * total], chosen), onehot(behind))
    weight_far = jnp.zeros((total, lanes), jnp.float32)
    for d in range(halo):
        weight_far = weight_far + jnp.where(at_k == d, others[d * total : (d + 1) * total], 0.0)

    def apply(x):
        rows = product(spread, x)
        expanded = product(
            jnp.concatenate([rows[d * total : (d + 1) * total] * mine for d in range(halo)], axis=0), far
        )
        own = product(rows[halo * total :], near)
        first, second = jnp.zeros((total, lanes), jnp.float32), jnp.zeros((total, lanes), jnp.float32)
        back = []
        for q in range(3):
            other = jnp.zeros((total, lanes), jnp.float32)
            for d in range(halo):
                piece = expanded[d * total : (d + 1) * total, q * lanes : (q + 1) * lanes]
                other = other + jnp.where(at_k == d, piece, 0.0)
            first = first + picks[q] * other
            second = second + picks[3 + q] * other
            back.append((picks[q] * own[:, :lanes] + picks[3 + q] * own[:, lanes:]) * weight_far)
        forward = jnp.concatenate([first * weight_near, second * weight_near], axis=1)
        forward = product_nt(forward, near)
        back = jnp.concatenate(back, axis=1)
        at_k3 = jnp.concatenate([at_k] * 3, axis=1)
        back = product_nt(
            jnp.concatenate([jnp.where(at_k3 == d, back, 0.0) for d in range(halo)], axis=0), far
        )
        stacked = [back[d * total : (d + 1) * total] * mine for d in range(halo)] + [forward]
        stacked = jnp.concatenate(stacked, axis=0)
        return lax.dot_general(
            spread, stacked, (((0,), (0,)), ((), ())), precision=HIGHEST,
            preferred_element_type=jnp.float32,
        )

    def normalize(raw):
        mean = jnp.sum(raw * raw) / float(nblk * entries)
        return raw / jnp.sqrt(mean + norm_eps)

    one = normalize(apply(start))
    two = normalize(apply(one))
    return one, two


def kernel(
    nblk, ncols, lines,
    counts_ref, partners_ref, start_ref, images_ref, const_ref,
    one_ref, two_ref,
    recv, images, own, pick, pad, gathered, result, other, s0, s1, s2, s3, left, packet, send_sem, recv_sem, psend_sem, precv_sem, local_sem,
):
    scores = (s0, s1, s2, s3)
    count = images_ref.shape[0]
    share = count // ncols
    fetch = recv.shape[0]
    halo = fetch // share
    slots = partners_ref.shape[1]
    width = other.shape[0]
    rows = own.shape[1] // 4
    half_images = count // 2
    row = lax.axis_index("rows")
    col = lax.axis_index("cols")
    me = row * ncols + col
    total = nblk * ncols
    ring = nblk == 2 * halo

    sends = []
    for k in range(1, halo + 1):
        for b in range(share):
            f = (k - 1) * share + b
            target = lax.rem(row - k + nblk, nblk)
            copy = pltpu.make_async_remote_copy(
                src_ref=images_ref.at[col * share + b],
                dst_ref=recv.at[f],
                send_sem=send_sem.at[f],
                recv_sem=recv_sem.at[f],
                device_id=(target, col),
                device_id_type=MESH,
            )
            copy.start()
            sends.append(copy)

    local = pltpu.make_async_copy(images_ref, images, local_sem)
    local.start()
    left[...] = jnp.zeros_like(left)
    table_at = 3 * rows + 32
    pick_at = table_at + 16 * width // 128
    order = const_ref[pick_at : pick_at + 4 * rows, :]
    order = jnp.concatenate([order] * (width // 128), axis=1).astype(jnp.int32)[:, :lines]
    pick[...] = onehot(order == iota((4 * rows, lines), 1), jnp.bfloat16)
    pad[...] = onehot(iota((width, lines), 0) == iota((width, lines), 1), jnp.bfloat16)
    local.wait()

    @pl.loop(0, count)
    def _(a):
        own[a] = jnp.dot(pick[...], images[a], preferred_element_type=jnp.float32).astype(jnp.bfloat16)

    def wide(at):
        return jnp.concatenate([const_ref[at : at + 8, :]] * (width // 128), axis=1)

    scale = score_gain * math.log2(math.e)
    lane = lax.broadcasted_iota(jnp.int32, (8, width), 1)
    side = jnp.where(row >= nblk // 2, 1, 0)
    high = jnp.where(col >= ncols // 2, 1, 0)
    mixed = lax.rem(side + high, 2)
    split = fetch - share if ring else fetch
    units = 2 * split + (fetch - split)

    def unit(u, carry):
        f = jnp.where(u < 2 * split, u // 2, u - split)
        h = jnp.where(u < 2 * split, lax.rem(u, 2), mixed)
        fresh = jnp.where(u < 2 * split, 1 - lax.rem(u, 2), 1)

        @pl.when(fresh == 1)
        def _():
            pltpu.make_async_copy(recv.at[f], recv.at[f], recv_sem.at[f]).wait()
            other[...] = jnp.dot(
                pad[...], recv[f], preferred_element_type=jnp.float32
            ).astype(jnp.bfloat16)

        for i in range(half_images):
            s_ref = scores[i]
            a = h * half_images + i
            s = lax.dot_general(
                own[a], other[...], (((1,), (1,)), ((), ())), preferred_element_type=jnp.float32
            )
            s_ref[...] = s
            top = jnp.max(s.reshape(4 * rows // 8, 8, width), axis=0)
            acc = [jnp.zeros((8, width), jnp.float32) for _ in range(4)]
            for g in range(rows // 8):
                w = []
                for j in range(4):
                    part = s_ref[j * rows + g * 8 : j * rows + g * 8 + 8, :]
                    part = jnp.exp2((part - top) * scale)
                    if g == rows // 8 - 1:
                        part = part * wide(3 * rows + 8 * j)
                    w.append(part)
                s14, d14 = w[0] + w[3], w[0] - w[3]
                s23, d23 = w[1] + w[2], w[1] - w[2]
                both = s14 + s23
                acc[0] = acc[0] + (s14 - s23) * wide(0 * rows + g * 8)
                acc[1] = acc[1] + (d14 + d23) * wide(1 * rows + g * 8)
                acc[2] = acc[2] + both * wide(2 * rows + g * 8)
                acc[3] = acc[3] + both
            masked = jnp.where(lane < lines, top, -jnp.inf)
            peak = jnp.max(masked)
            factor = jnp.exp2((masked - peak) * scale)
            for p in range(4):
                left[p, pl.ds(f * count + a, 1), :] = jnp.sum(acc[p] * factor, axis=0, keepdims=True)
        return carry

    lax.fori_loop(0, units, unit, 0)

    npair = fetch * count
    table = const_ref[table_at:pick_at, :].reshape(2, 8, width)
    first = product_nt(table[0], left[0:2].reshape(2 * npair, width))
    second = product_nt(table[1], left[2:4].reshape(2 * npair, width))
    sums = second[6:7, npair:]
    sums = jnp.concatenate([sums, sums], axis=1)
    inverse = jnp.where(sums > 0.0, 1.0 / sums, 0.0)
    prow = lax.broadcasted_iota(jnp.int32, (8, 2 * npair), 0)
    plane = lax.broadcasted_iota(jnp.int32, (8, 2 * npair), 1)
    value = jnp.where(prow < 3, first, jnp.where(prow < 6, second, 0.0)) * inverse
    valid = jnp.zeros((8, 2 * npair), jnp.float32)
    for s in range(slots):
        on = jnp.where(counts_ref[0] > s, 1.0, 0.0)
        valid = valid + jnp.where(plane == partners_ref[0, s], on, 0.0)
    packet[...] = jnp.where(prow == 6, valid, value)
    packet[7:8, :] = jnp.zeros((1, 2 * npair), jnp.float32)
    packet[7:8, 0 : start_ref.shape[1]] = start_ref[...]
    gathered[me] = packet[...]

    def give(t, carry):
        target = lax.rem(me + t, total)
        pltpu.make_async_remote_copy(
            src_ref=packet,
            dst_ref=gathered.at[me],
            send_sem=psend_sem,
            recv_sem=precv_sem,
            device_id=(target // ncols, lax.rem(target, ncols)),
            device_id_type=MESH,
        ).start()
        return carry

    lax.fori_loop(1, total, give, 0)
    for copy in sends:
        copy.wait_send()
    everyone = gathered.at[pl.ds(0, total - 1)]
    pltpu.make_async_copy(everyone, everyone, psend_sem).wait()
    pltpu.make_async_copy(everyone, everyone, precv_sem).wait()

    one, two = iterate(gathered, nblk, ncols, halo, share, count, slots)
    result[0] = one
    result[1] = two
    entries = one_ref.shape[1]
    one_ref[...] = result[0, pl.ds(row, 1), :][:, :entries]
    two_ref[...] = result[1, pl.ds(row, 1), :][:, :entries]


def body(images, partners, counts, start):
    count, lines, radii = images.shape
    slots = partners.shape[1]
    halo = slots // 2
    ncols = lax.axis_size("cols")
    nblk = lax.axis_size("rows")
    share = count // ncols
    width = (lines + 127) // 128 * 128
    const = constants(lines, width)
    rows4 = (lines // 4 + 8) // 8 * 32
    total = nblk * ncols
    npair = halo * share * count
    vmem = pl.BlockSpec(memory_space=pltpu.VMEM)
    smem = pl.BlockSpec(memory_space=pltpu.SMEM)
    hbm = pl.BlockSpec(memory_space=pl.ANY)
    shape = jax.ShapeDtypeStruct((1, 3 * count), jnp.float32)
    return pl.pallas_call(
        functools.partial(kernel, nblk, ncols, lines),
        out_shape=(shape, shape),
        in_specs=[smem, smem, vmem, hbm, vmem],
        out_specs=(vmem, vmem),
        scratch_shapes=[
            pltpu.VMEM((halo * share, lines, radii), jnp.bfloat16),
            pltpu.VMEM((count, lines, radii), jnp.bfloat16),
            pltpu.VMEM((count, rows4, radii), jnp.bfloat16),
            pltpu.VMEM((rows4, lines), jnp.bfloat16),
            pltpu.VMEM((width, lines), jnp.bfloat16),
            pltpu.VMEM((total, 8, 2 * npair), jnp.float32),
            pltpu.VMEM((2, nblk, 128), jnp.float32),
            pltpu.VMEM((width, radii), jnp.bfloat16),
            pltpu.VMEM((rows4, width), jnp.float32),
            pltpu.VMEM((rows4, width), jnp.float32),
            pltpu.VMEM((rows4, width), jnp.float32),
            pltpu.VMEM((rows4, width), jnp.float32),
            pltpu.VMEM((4, npair, width), jnp.float32),
            pltpu.VMEM((8, 2 * npair), jnp.float32),
            pltpu.SemaphoreType.DMA((halo * share,)),
            pltpu.SemaphoreType.DMA((halo * share,)),
            pltpu.SemaphoreType.DMA,
            pltpu.SemaphoreType.DMA,
            pltpu.SemaphoreType.DMA,
        ],
        compiler_params=pltpu.CompilerParams(has_side_effects=True, vmem_limit_bytes=48 * 2**20),
    )(counts, partners, start, images, jnp.asarray(const))


def solution(mesh):
    in_specs = (P("rows", None, None), P("rows", None), P("rows"), P("rows", None))
    out_specs = (P("rows", None), P("rows", None))
    return jax.shard_map(body, mesh=mesh, in_specs=in_specs, out_specs=out_specs, check_vma=False)
```

time: 105 us -> 49.6 us (0.47)
  matrix products: 41.5 us -> 0 us
  local copies, waits for them, and re-layouts: 13.7 us -> 3.13 us
  other arithmetic: 4.59 us -> 0 us
  Pallas kernels: 41.6 us -> 45 us
  between operations: 2.89 us -> 1.34 us
    dot_general x1 -> x0, matrix products: 41.5 us -> none  [apply(): back = jnp.einsum('icpqkba,ipa->ikqcb', rel, x, precision=HIGHEST)]
    unnamed x23 -> x10, local copies, waits for them, and re-layouts: 8.75 us -> 3.13 us
    pallas_call x1, Pallas kernels: 41.6 us -> 45 us  [body(): pl.pallas_call(functools.partial(kernel, nblk, ncols, lines), out_shape=(...]
    unnamed x6 -> x0, other arithmetic: 2.42 us -> none
    slice x40 -> x0, local copies, waits for them, and re-layouts: 1.89 us -> none  [the longest x19 1.04 us: apply(): jnp.roll(split, -k, axis=0)]
    another operation x5 -> x0, local copies, waits for them, and re-layouts: 1.77 us -> none  [the longest x4 1.69 us: body(): jnp.stack([packets[:, 0:3, :npair], packets[:, 0:3, npair:], packets[:, 3...]
    reduce_sum x2 -> x0, other arithmetic: 1.4 us -> none  [normalize(): return raw / jnp.sqrt(jnp.mean(raw * raw) + norm_eps)]
where the time goes in v2:
time: 49.6 us; the launch traced here: 49.4 us
  Pallas kernels  45 us (91%)
  local copies, waits for them, and re-layouts  3.13 us (6%)
  between operations  1.34 us (3%)
    pallas_call x1, Pallas kernels, body(): pl.pallas_call(functools.partial(kernel, nblk, ncols, lines), out_shape=(...  45 us
    unnamed x10, local copies, waits for them, and re-layouts  3.13 us

profile of v2, /device:TPU:0, one launch (start us, length us, event | category | flops | bytes accessed | tf_op | source)
XLA Modules:
  0.0 49.4 jit_solution(1357650969996926115)
XLA Ops:
  0.6 0.0 copy-start.3
  0.6 0.0 copy-start.2
  1.3 0.0 copy-done.3
  1.3 0.0 copy-done.2
  1.3 0.0 copy-start
  1.3 1.1 %copy-done = bf16[8,360,128]{2,1,0:T(8,128)(2,1)S(1)} copy-done((bf16[8,360,128]{2,1,0:T(8,128)(2,1)S(1)}, bf16[8,360,128]{2,1,0:T(8,128)(2,1)}, u32[]{:S(2)}) %copy-start) | copy-done | bytes 737304
  2.5 0.0 copy-start.1
  2.5 1.0 %copy-done.1 = f32[752,128]{1,0:T(8,128)S(1)} copy-done((f32[752,128]{1,0:T(8,128)S(1)}, f32[752,128]{1,0:T(8,128)}, u32[]{:S(2)}) %copy-start.1) | copy-done | bytes 385048
  3.4 45.0 %shard_map.68 = (f32[1,24]{1,0:T(1,128)S(1)}, f32[1,24]{1,0:T(1,128)S(1)}) custom-call(s32[1]{0:T(128)S(6)} %copy.9.counts_ref, s32[1,8]{1,0:T(1,128)S(1)} %copy-done.2, f32[1,24]{1,0:T(1,128)S(1)} %copy-done.3, bf16[8,360,128]{2,1,0:T(8,128)(2,1)S(1)} %copy-done, f32[752,128]{1,0:T(8,128)S(1)} %copy-done.1), custom_call_target="tpu_custom_call" | custom-call | tf_op jit(solution)/shard_map/pallas_call | solution.py:316
  48.4 0.5 %copy.10 = f32[1,24]{1,0:T(1,128)} copy(f32[1,24]{1,0:T(1,128)S(1)} %get-tuple-element.4) | data formatting | bytes 192
  48.9 0.5 %copy.11 = f32[1,24]{1,0:T(1,128)} copy(f32[1,24]{1,0:T(1,128)S(1)} %get-tuple-element.5) | data formatting | bytes 192
Async XLA Ops:
  0.6 0.7 %copy-start.3 = (f32[1,24]{1,0:T(1,128)S(1)}, f32[1,24]{1,0:T(1,128)}, u32[]{:S(2)}) copy-start(f32[1,24]{1,0:T(1,128)} %start_ref.1) | copy-start | bytes 292
  0.6 0.7 %copy-start.2 = (s32[1,8]{1,0:T(1,128)S(1)}, s32[1,8]{1,0:T(1,128)}, u32[]{:S(2)}) copy-start(s32[1,8]{1,0:T(1,128)} %partners_ref.1) | copy-start | bytes 100
  1.3 1.1 %copy-start = (bf16[8,360,128]{2,1,0:T(8,128)(2,1)S(1)}, bf16[8,360,128]{2,1,0:T(8,128)(2,1)}, u32[]{:S(2)}) copy-start(bf16[8,360,128]{2,1,0:T(8,128)(2,1)} %images_ref.1) | copy-start | bytes 2211844
  2.5 1.0 %copy-start.1 = (f32[752,128]{1,0:T(8,128)S(1)}, f32[752,128]{1,0:T(8,128)}, u32[]{:S(2)}) copy-start(f32[752,128]{1,0:T(8,128)} %constant.2.clone.const_ref) | copy-start | bytes 1155076

commit v3 on v2

--- a/solution.py
+++ b/solution.py
@@ -64,9 +64,16 @@
     )
 
 
-def iterate(gathered, nblk, ncols, halo, share, count, slots):
+def ahead_of(block, step, nblk, halo):
+    if nblk != 2 * halo:
+        return (block + step + nblk) % nblk
+    half = nblk // 2
+    place = (block % 2 * half + block // 2 + step + nblk) % nblk
+    return place % half * 2 + place // half
+
+
+def iterate(gathered, nblk, ncols, halo, share, count):
     total = nblk * ncols
-    ring = nblk == 2 * halo
     npair = halo * share * count
     lanes = 2 * npair
     entries = 3 * count
@@ -80,7 +87,7 @@
     k = iota((place, nblk), 0) // total
     block = iota((place, nblk), 0) % total // ncols
     step = jnp.where(k < halo, k + 1, 0)
-    spread = onehot(iota((place, nblk), 1) == (block + step) % nblk)
+    spread = onehot(iota((place, nblk), 1) == ahead_of(block, step, nblk, halo))
     entry = iota((total, 128), 1)
     owner = iota((total, 128), 0) % ncols
     mine = onehot((entry < entries) & (entry % count // share == owner))
@@ -91,18 +98,18 @@
     r, c = iota((128, 2 * lanes), 0), iota((128, 2 * lanes), 1)
     part = c // npair
     near = onehot((r < entries) & (r % count == c % count) & (r // count == part))
-    code, k2 = iota((128, lanes), 0), iota((128, lanes), 1) % npair // (share * count)
-    ahead = code == halo + k2
-    behind = code == halo - 1 - k2
-    if ring:
-        ahead = ahead | ((code == 0) & (k2 == halo - 1))
-        behind = behind | ((code == slots - 1) & (k2 == halo - 1))
     here = product(spread[halo * total :], chosen)
-    weight_near = product(here, onehot(ahead))
-    others = product(product(spread[: halo * total], chosen), onehot(behind))
+    others = product(spread[: halo * total], chosen)
+    home = iota((total, 128), 0) // ncols
+    back_home = onehot(entry == home)
+    weight_near = jnp.zeros((total, lanes), jnp.float32)
     weight_far = jnp.zeros((total, lanes), jnp.float32)
     for d in range(halo):
-        weight_far = weight_far + jnp.where(at_k == d, others[d * total : (d + 1) * total], 0.0)
+        there = onehot(entry == ahead_of(home, d + 1, nblk, halo))
+        given = jnp.sum(here * there, axis=1, keepdims=True)
+        taken = jnp.sum(others[d * total : (d + 1) * total] * back_home, axis=1, keepdims=True)
+        weight_near = weight_near + jnp.where(at_k == d, given, 0.0)
+        weight_far = weight_far + jnp.where(at_k == d, taken, 0.0)
 
     def apply(x):
         rows = product(spread, x)
@@ -147,7 +154,7 @@
     nblk, ncols, lines,
     counts_ref, partners_ref, start_ref, images_ref, const_ref,
     one_ref, two_ref,
-    recv, images, own, pick, pad, gathered, result, other, s0, s1, s2, s3, left, packet, send_sem, recv_sem, psend_sem, precv_sem, local_sem,
+    recv, images, own, pick, pad, gathered, result, other, s0, s1, s2, s3, left, packet, send_sem, recv_sem, psend_sem, precv_sem, gsend_sem, grecv_sem, local_sem,
 ):
     scores = (s0, s1, s2, s3)
     count = images_ref.shape[0]
@@ -168,7 +175,7 @@
     for k in range(1, halo + 1):
         for b in range(share):
             f = (k - 1) * share + b
-            target = lax.rem(row - k + nblk, nblk)
+            target = ahead_of(row, -k, nblk, halo)
             copy = pltpu.make_async_remote_copy(
                 src_ref=images_ref.at[col * share + b],
                 dst_ref=recv.at[f],
@@ -200,7 +207,7 @@
 
     scale = score_gain * math.log2(math.e)
     lane = lax.broadcasted_iota(jnp.int32, (8, width), 1)
-    side = jnp.where(row >= nblk // 2, 1, 0)
+    side = lax.rem(row, 2)
     high = jnp.where(col >= ncols // 2, 1, 0)
     mixed = lax.rem(side + high, 2)
     split = fetch - share if ring else fetch
@@ -264,32 +271,41 @@
     valid = jnp.zeros((8, 2 * npair), jnp.float32)
     for s in range(slots):
         on = jnp.where(counts_ref[0] > s, 1.0, 0.0)
-        valid = valid + jnp.where(plane == partners_ref[0, s], on, 0.0)
+        code = partners_ref[0, s]
+        offset = jnp.where(code < halo, code - halo, code - halo + 1)
+        valid = valid + jnp.where(plane == lax.rem(row + offset + nblk, nblk), on, 0.0)
     packet[...] = jnp.where(prow == 6, valid, value)
     packet[7:8, :] = jnp.zeros((1, 2 * npair), jnp.float32)
     packet[7:8, 0 : start_ref.shape[1]] = start_ref[...]
     gathered[me] = packet[...]
 
-    def give(t, carry):
-        target = lax.rem(me + t, total)
+    def give(source, target, device, send, recv):
         pltpu.make_async_remote_copy(
-            src_ref=packet,
-            dst_ref=gathered.at[me],
-            send_sem=psend_sem,
-            recv_sem=precv_sem,
-            device_id=(target // ncols, lax.rem(target, ncols)),
-            device_id_type=MESH,
+            src_ref=source, dst_ref=target, send_sem=send, recv_sem=recv,
+            device_id=device, device_id_type=MESH,
         ).start()
+
+    def settle(size, sem):
+        some = gathered.at[pl.ds(0, size)]
+        pltpu.make_async_copy(some, some, sem).wait()
+
+    for t in range(1, ncols):
+        give(packet, gathered.at[me], (row, lax.rem(col + t, ncols)), psend_sem, precv_sem)
+    settle(ncols - 1, precv_sem)
+    group = gathered.at[pl.ds(row * ncols, ncols)]
+
+    def give_row(t, carry):
+        give(group, group, (lax.rem(row + t, nblk), col), gsend_sem, grecv_sem)
         return carry
 
-    lax.fori_loop(1, total, give, 0)
+    lax.fori_loop(1, nblk, give_row, 0)
     for copy in sends:
         copy.wait_send()
-    everyone = gathered.at[pl.ds(0, total - 1)]
-    pltpu.make_async_copy(everyone, everyone, psend_sem).wait()
-    pltpu.make_async_copy(everyone, everyone, precv_sem).wait()
-
-    one, two = iterate(gathered, nblk, ncols, halo, share, count, slots)
+    settle(ncols - 1, psend_sem)
+    settle((nblk - 1) * ncols, gsend_sem)
+    settle((nblk - 1) * ncols, grecv_sem)
+
+    one, two = iterate(gathered, nblk, ncols, halo, share, count)
     result[0] = one
     result[1] = two
     entries = one_ref.shape[1]
@@ -338,6 +354,8 @@
             pltpu.SemaphoreType.DMA,
             pltpu.SemaphoreType.DMA,
             pltpu.SemaphoreType.DMA,
+            pltpu.SemaphoreType.DMA,
+            pltpu.SemaphoreType.DMA,
         ],
         compiler_params=pltpu.CompilerParams(has_side_effects=True, vmem_limit_bytes=48 * 2**20),
     )(counts, partners, start, images, jnp.asarray(const))

time: 49.6 us -> 52 us (1.048)
  Pallas kernels: 45 us -> 47.3 us
    pallas_call x1, Pallas kernels: 45 us -> 47.3 us  [body(): pl.pallas_call(functools.partial(kernel, nblk, ncols, lines), out_shape=(...]
where the time goes in v3:
time: 52 us; the launch traced here: 51.8 us
  Pallas kernels  47.3 us (91%)
  local copies, waits for them, and re-layouts  3.13 us (6%)
  between operations  1.34 us (3%)
    pallas_call x1, Pallas kernels, body(): pl.pallas_call(functools.partial(kernel, nblk, ncols, lines), out_shape=(...  47.3 us
    unnamed x10, local copies, waits for them, and re-layouts  3.13 us

profile of v3, /device:TPU:0, one launch (start us, length us, event | category | flops | bytes accessed | tf_op | source)
XLA Modules:
  0.0 51.8 jit_solution(6288090570410632754)
XLA Ops:
  0.6 0.0 copy-start.3
  0.6 0.0 copy-start.2
  1.3 0.0 copy-done.3
  1.3 0.0 copy-done.2
  1.3 0.0 copy-start
  1.3 1.1 %copy-done = bf16[8,360,128]{2,1,0:T(8,128)(2,1)S(1)} copy-done((bf16[8,360,128]{2,1,0:T(8,128)(2,1)S(1)}, bf16[8,360,128]{2,1,0:T(8,128)(2,1)}, u32[]{:S(2)}) %copy-start) | copy-done | bytes 737304
  2.5 0.0 copy-start.1
  2.5 1.0 %copy-done.1 = f32[752,128]{1,0:T(8,128)S(1)} copy-done((f32[752,128]{1,0:T(8,128)S(1)}, f32[752,128]{1,0:T(8,128)}, u32[]{:S(2)}) %copy-start.1) | copy-done | bytes 385048
  3.4 47.3 %shard_map.68 = (f32[1,24]{1,0:T(1,128)S(1)}, f32[1,24]{1,0:T(1,128)S(1)}) custom-call(s32[1]{0:T(128)S(6)} %copy.9.counts_ref, s32[1,8]{1,0:T(1,128)S(1)} %copy-done.2, f32[1,24]{1,0:T(1,128)S(1)} %copy-done.3, bf16[8,360,128]{2,1,0:T(8,128)(2,1)S(1)} %copy-done, f32[752,128]{1,0:T(8,128)S(1)} %copy-done.1), custom_call_target="tpu_custom_call" | custom-call | tf_op jit(solution)/shard_map/pallas_call | solution.py:332
  50.8 0.5 copy.10
  51.3 0.5 copy.11
Async XLA Ops:
  0.6 0.7 %copy-start.3 = (f32[1,24]{1,0:T(1,128)S(1)}, f32[1,24]{1,0:T(1,128)}, u32[]{:S(2)}) copy-start(f32[1,24]{1,0:T(1,128)} %start_ref.1) | copy-start | bytes 292
  0.6 0.7 %copy-start.2 = (s32[1,8]{1,0:T(1,128)S(1)}, s32[1,8]{1,0:T(1,128)}, u32[]{:S(2)}) copy-start(s32[1,8]{1,0:T(1,128)} %partners_ref.1) | copy-start | bytes 100
  1.3 1.1 %copy-start = (bf16[8,360,128]{2,1,0:T(8,128)(2,1)S(1)}, bf16[8,360,128]{2,1,0:T(8,128)(2,1)}, u32[]{:S(2)}) copy-start(bf16[8,360,128]{2,1,0:T(8,128)(2,1)} %images_ref.1) | copy-start | bytes 2211844
  2.5 1.0 %copy-start.1 = (f32[752,128]{1,0:T(8,128)S(1)}, f32[752,128]{1,0:T(8,128)}, u32[]{:S(2)}) copy-start(f32[752,128]{1,0:T(8,128)} %constant.2.clone.const_ref) | copy-start | bytes 1155076

commit v4 on v2

--- a/solution.py
+++ b/solution.py
@@ -147,7 +147,7 @@
     nblk, ncols, lines,
     counts_ref, partners_ref, start_ref, images_ref, const_ref,
     one_ref, two_ref,
-    recv, images, own, pick, pad, gathered, result, other, s0, s1, s2, s3, left, packet, send_sem, recv_sem, psend_sem, precv_sem, local_sem,
+    recv, images, own, pick, pad, gathered, result, other, s0, s1, s2, s3, left, packet, send_sem, recv_sem, psend_sem, precv_sem, gsend_sem, grecv_sem, local_sem,
 ):
     scores = (s0, s1, s2, s3)
     count = images_ref.shape[0]
@@ -270,24 +270,31 @@
     packet[7:8, 0 : start_ref.shape[1]] = start_ref[...]
     gathered[me] = packet[...]
 
-    def give(t, carry):
-        target = lax.rem(me + t, total)
+    def give(source, target, device, send, recv):
         pltpu.make_async_remote_copy(
-            src_ref=packet,
-            dst_ref=gathered.at[me],
-            send_sem=psend_sem,
-            recv_sem=precv_sem,
-            device_id=(target // ncols, lax.rem(target, ncols)),
-            device_id_type=MESH,
+            src_ref=source, dst_ref=target, send_sem=send, recv_sem=recv,
+            device_id=device, device_id_type=MESH,
         ).start()
+
+    def settle(size, sem):
+        some = gathered.at[pl.ds(0, size)]
+        pltpu.make_async_copy(some, some, sem).wait()
+
+    for t in range(1, ncols):
+        give(packet, gathered.at[me], (row, lax.rem(col + t, ncols)), psend_sem, precv_sem)
+    settle(ncols - 1, precv_sem)
+    group = gathered.at[pl.ds(row * ncols, ncols)]
+
+    def give_row(t, carry):
+        give(group, group, (lax.rem(row + t, nblk), col), gsend_sem, grecv_sem)
         return carry
 
-    lax.fori_loop(1, total, give, 0)
+    lax.fori_loop(1, nblk, give_row, 0)
     for copy in sends:
         copy.wait_send()
-    everyone = gathered.at[pl.ds(0, total - 1)]
-    pltpu.make_async_copy(everyone, everyone, psend_sem).wait()
-    pltpu.make_async_copy(everyone, everyone, precv_sem).wait()
+    settle(ncols - 1, psend_sem)
+    settle((nblk - 1) * ncols, gsend_sem)
+    settle((nblk - 1) * ncols, grecv_sem)
 
     one, two = iterate(gathered, nblk, ncols, halo, share, count, slots)
     result[0] = one
@@ -338,6 +345,8 @@
             pltpu.SemaphoreType.DMA,
             pltpu.SemaphoreType.DMA,
             pltpu.SemaphoreType.DMA,
+            pltpu.SemaphoreType.DMA,
+            pltpu.SemaphoreType.DMA,
         ],
         compiler_params=pltpu.CompilerParams(has_side_effects=True, vmem_limit_bytes=48 * 2**20),
     )(counts, partners, start, images, jnp.asarray(const))

time: 49.6 us -> 52 us (1.048)
  Pallas kernels: 45 us -> 47.3 us
    pallas_call x1, Pallas kernels: 45 us -> 47.3 us  [body(): pl.pallas_call(functools.partial(kernel, nblk, ncols, lines), out_shape=(...]
where the time goes in v4:
time: 52 us; the launch traced here: 51.8 us
  Pallas kernels  47.3 us (91%)
  local copies, waits for them, and re-layouts  3.13 us (6%)
  between operations  1.34 us (3%)
    pallas_call x1, Pallas kernels, body(): pl.pallas_call(functools.partial(kernel, nblk, ncols, lines), out_shape=(...  47.3 us
    unnamed x10, local copies, waits for them, and re-layouts  3.13 us

profile of v4, /device:TPU:0, one launch (start us, length us, event | category | flops | bytes accessed | tf_op | source)
XLA Modules:
  0.0 51.8 jit_solution(15623042441829463352)
XLA Ops:
  0.6 0.0 copy-start.3
  0.6 0.0 copy-start.2
  1.3 0.0 copy-done.3
  1.3 0.0 copy-done.2
  1.3 0.0 copy-start
  1.3 1.1 %copy-done = bf16[8,360,128]{2,1,0:T(8,128)(2,1)S(1)} copy-done((bf16[8,360,128]{2,1,0:T(8,128)(2,1)S(1)}, bf16[8,360,128]{2,1,0:T(8,128)(2,1)}, u32[]{:S(2)}) %copy-start) | copy-done | bytes 737304
  2.5 0.0 copy-start.1
  2.5 1.0 %copy-done.1 = f32[752,128]{1,0:T(8,128)S(1)} copy-done((f32[752,128]{1,0:T(8,128)S(1)}, f32[752,128]{1,0:T(8,128)}, u32[]{:S(2)}) %copy-start.1) | copy-done | bytes 385048
  3.4 47.3 %shard_map.68 = (f32[1,24]{1,0:T(1,128)S(1)}, f32[1,24]{1,0:T(1,128)S(1)}) custom-call(s32[1]{0:T(128)S(6)} %copy.9.counts_ref, s32[1,8]{1,0:T(1,128)S(1)} %copy-done.2, f32[1,24]{1,0:T(1,128)S(1)} %copy-done.3, bf16[8,360,128]{2,1,0:T(8,128)(2,1)S(1)} %copy-done, f32[752,128]{1,0:T(8,128)S(1)} %copy-done.1), custom_call_target="tpu_custom_call" | custom-call | tf_op jit(solution)/shard_map/pallas_call | solution.py:323
  50.7 0.5 copy.10
  51.3 0.5 copy.11
Async XLA Ops:
  0.6 0.7 %copy-start.3 = (f32[1,24]{1,0:T(1,128)S(1)}, f32[1,24]{1,0:T(1,128)}, u32[]{:S(2)}) copy-start(f32[1,24]{1,0:T(1,128)} %start_ref.1) | copy-start | bytes 292
  0.6 0.7 %copy-start.2 = (s32[1,8]{1,0:T(1,128)S(1)}, s32[1,8]{1,0:T(1,128)}, u32[]{:S(2)}) copy-start(s32[1,8]{1,0:T(1,128)} %partners_ref.1) | copy-start | bytes 100
  1.3 1.1 %copy-start = (bf16[8,360,128]{2,1,0:T(8,128)(2,1)S(1)}, bf16[8,360,128]{2,1,0:T(8,128)(2,1)}, u32[]{:S(2)}) copy-start(bf16[8,360,128]{2,1,0:T(8,128)(2,1)} %images_ref.1) | copy-start | bytes 2211844
  2.5 1.0 %copy-start.1 = (f32[752,128]{1,0:T(8,128)S(1)}, f32[752,128]{1,0:T(8,128)}, u32[]{:S(2)}) copy-start(f32[752,128]{1,0:T(8,128)} %constant.2.clone.const_ref) | copy-start | bytes 1155076
